TPU v7x, 32 devices: a whole 2x2x4 slice. The times are simulated.
32 devices in a mesh: row: 8 (over z, x), col: 4 (over y, core).
Axes of the slice: x: 2, y: 2, z: 4, core: 2. Of those that a mesh axis runs over, the one named last changes fastest.
Arguments:
- tokens: bfloat16 [3008, 8192], P('row', 'col'), may hold values from -6 to 6
- weight: bfloat16 [8192, 26624], P('row', 'col'), may hold values from -0.0625 to 0.0625
Outputs:
- activated: bfloat16 [3008, 26624], P('row', 'col')
All inputs are finite; a program needn't handle non-finite values.
Results may differ from a plain program's by a relative error of at most 0.001.
Values may be sent and summed in bfloat16 or wider, within the bound.
A program may use at most 192 MiB of HBM per device.

v0:
```python
import jax
import jax.numpy as jnp
from jax import lax
from jax.sharding import PartitionSpec as P


def on_device(tokens, weight):
    whole_weight = lax.all_gather(weight, "row", axis=0, tiled=True)
    preact = jnp.dot(
        lax.all_gather(tokens, "col", axis=1, tiled=True),
        whole_weight,
        preferred_element_type=jnp.float32,
    )
    return jax.nn.silu(preact).astype(jnp.bfloat16)


def solution(mesh):
    placed = (P("row", "col"), P("row", "col"))
    return jax.shard_map(
        on_device, mesh=mesh, in_specs=placed, out_specs=P("row", "col"), check_vma=False
    )
```

profile of v0, /device:TPU:0, one launch (start us, length us, event | category | flops | bytes accessed | tf_op | source)
XLA Modules:
  0.0 2177.6 jit_solution(4488159543270625522)
XLA Ops:
  6.5 0.0 all-gather.3.cloned.1.call-start
  6.5 0.7 all-gather.3.cloned.1.call-update
  7.3 0.0 all-gather.5.cloned.1.call-start
  7.3 0.7 all-gather.5.cloned.1.call-update
  8.0 49.3 %all-gather.3.cloned.1.call-done = bf16[376,8192]{1,0:T(8,128)(2,1)} async-done(((bf16[376,2048]{1,0:T(8,128)(2,1)}), bf16[376,8192]{1,0:T(8,128)(2,1)}) %all-gather.3.cloned.1.call-update) | async-done | bytes 6160400 | tf_op jit(solution)/shard_map/all_gather | solution.py:10
  57.3 2054.9 %all-gather.5.cloned.1.call-done = bf16[8192,6656]{1,0:T(8,128)(2,1)} async-done(((bf16[1024,6656]{1,0:T(8,128)(2,1)}), bf16[8192,6656]{1,0:T(8,128)(2,1)}) %all-gather.5.cloned.1.call-update) | async-done | bytes 109051920 | tf_op jit(solution)/shard_map/all_gather | solution.py:8
  2112.2 58.5 %multiply_convert_fusion = bf16[376,6656]{1,0:T(8,128)(2,1)} fusion(bf16[376,8192]{1,0:T(8,128)(2,1)} %all-gather.3.cloned.1.call-done, bf16[8192,6656]{1,0:T(8,128)(2,1)} %all-gather.5.cloned.1.call-done), kind=kOutput, calls=%fused_computation | convolution fusion | flops 41016029184 | bytes 120217600 | tf_op jit(solution)/shard_map/dot_general | solution.py:9
Async XLA Ops:
  6.5 50.8 %all-gather.3.cloned.1.call-start = ((), (), s32[]{:S(2)}) async-start(), calls=%async_computation | async-start | bytes 7700480 | tf_op jit(solution)/shard_map/all_gather | solution.py:10
  7.3 2105.0 %all-gather.5.cloned.1.call-start = ((), (), s32[]{:S(2)}) async-start(), calls=%async_computation.1 | async-start | bytes 122683392 | tf_op jit(solution)/shard_map/all_gather | solution.py:8
Sparse Core Ops, SparseCore 0:
  8.9 48.3 all-gather.2
  58.8 2053.3 all-gather.4
where the time goes:
time: 2180 us
  waiting for transfers between devices  2110 us (97%)
  matrix products  58.5 us (3%)
    all_gather x1, waiting for transfers between devices, on_device(): whole_weight = lax.all_gather(weight, 'row', axis=0, tiled=True)  2050 us
    dot_general x1, matrix products, on_device(): jnp.dot(lax.all_gather(tokens, 'col', axis=1, tiled=True), whole_weight,...  58.5 us
    all_gather x1, waiting for transfers between devices, on_device(): lax.all_gather(tokens, 'col', axis=1, tiled=True)  49.3 us
  transfers between devices with their start and end apart: 2, of which 2 were waited for; matrix products, arithmetic and copies ran while one was open for 0% of the time, Pallas kernels for 0%

commit v1 on v0

v1 whole, which is shorter than its diff:
```python
import functools

import jax
import jax.numpy as jnp
from jax import lax
from jax.experimental import pallas as pl
from jax.experimental.pallas import tpu as pltpu
from jax.sharding import PartitionSpec as P

LANES = 128
MESH = pl.DeviceIdType.MESH
PARTS = (4, 2, 1)


def silu(v):
    return v / (1.0 + jnp.exp(-v))


def kernel(tok_ref, w_ref, o_ref, all_ref, w_a, w_b, w_c, st_a, st_b, st_c, tbuf, acc_a, acc_b, acc_c,
           tsend, trecv, wsend, wrecv, osend, orecv, local, load):
    rows = 8
    row, col = lax.axis_index("row"), lax.axis_index("col")
    z, x = row // 2, row % 2
    y, core = col // 2, col % 2
    depth = w_ref.shape[0]
    held, staged = (w_a, w_b, w_c), (st_a, st_b, st_c)
    base = sum(PARTS[:2])
    pair = 2 * base + 1

    z1 = z + 1 - 2 * (z % 2)
    half = z // 2
    near, far = 2 - half, 3 - 3 * half
    zmid = 3 - z
    inner = (z == 1) | (z == 2)
    to_z, to_mid = (z1 * 2 + x, col), (zmid * 2 + x, col)
    to_x = (z * 2 + 1 - x, col)
    to_y = (row, (1 - y) * 2 + core)
    to_core = (row, y * 2 + 1 - core)

    barrier = pltpu.get_barrier_semaphore()
    for k in range(1, rows):
        pl.semaphore_signal(barrier, inc=1, device_id=((row + k) % rows, col), device_id_type=MESH)
    pl.semaphore_signal(barrier, inc=1, device_id=to_y, device_id_type=MESH)
    pl.semaphore_signal(barrier, inc=1, device_id=to_core, device_id_type=MESH)
    pl.semaphore_wait(barrier, rows + 1)

    def tok(r, c, dst, slot, own=False):
        return pltpu.make_async_remote_copy(
            src_ref=tok_ref if own else all_ref.at[r, c],
            dst_ref=all_ref.at[r, c],
            send_sem=tsend.at[slot],
            recv_sem=trecv.at[r * 4 + c],
            device_id=dst,
            device_id_type=MESH,
        )

    zs = (z, z1, near, far)
    col_y, col_c, col_yc = (1 - y) * 2 + core, y * 2 + 1 - core, (1 - y) * 2 + 1 - core

    def z_sends(j):
        r = zs[j] * 2 + x
        own = j == 0
        if own:
            tok(r, col, to_z, 0, own).start()
        if j < 2:
            @pl.when(inner)
            def _():
                tok(r, col, to_mid, 1 + j, own).start()
        else:
            @pl.when(inner)
            def _():
                tok(r, col, to_z, 1 + j, own).start()
        tok(r, col, to_x, 5 + j, own).start()
        tok(r, col, to_y, 9 + 2 * j, own).start()
        tok(r, col, to_core, 17 + 4 * j, own).start()

    mine = pltpu.make_async_copy(tok_ref, all_ref.at[row, col], local.at[0])
    mine.start()
    z_sends(0)

    def first_col(p, part):
        at = pair * (p // 2) + (base + 1 - core) * (p % 2) + (0, PARTS[0], base)[part]
        return pl.multiple_of(at * LANES, LANES)

    def wide(p):
        return (p + core) % 2 == 0

    def when_held(part, p, run):
        if part < 2:
            run()
        else:
            pl.when(wide(p))(run)

    def w_copy(p, src, part):
        return pltpu.make_async_remote_copy(
            src_ref=w_ref.at[:, pl.ds(first_col(p, part), PARTS[part] * LANES)],
            dst_ref=held[part].at[src],
            send_sem=wsend.at[p * 3 + part],
            recv_sem=wrecv.at[src * 3 + part],
            device_id=(p, col),
            device_id_type=MESH,
        )

    def w_own(part):
        return pltpu.make_async_copy(
            w_ref.at[:, pl.ds(first_col(row, part), PARTS[part] * LANES)],
            held[part].at[row], local.at[1 + part])

    for part in (0, 2, 1):
        for k in (4, 2, 6, 3, 5, 1, 7):
            p = (row + k) % rows
            when_held(part, p, lambda p=p, part=part: w_copy(p, row, part).start())
        when_held(part, row, lambda part=part: w_own(part).start())

    for j in range(4):
        if j > 0:
            tok(zs[j] * 2 + x, col, to_z, 0).wait_recv()
            z_sends(j)
        r = zs[j] * 2 + 1 - x
        tok(r, col, to_x, 0).wait_recv()
        tok(r, col, to_y, 10 + 2 * j).start()
        tok(r, col, to_core, 19 + 4 * j).start()
    for j in range(4):
        for a in range(2):
            r = zs[j] * 2 + (x if a == 0 else 1 - x)
            tok(r, col_y, to_y, 0).wait_recv()
            tok(r, col_y, to_core, 18 + 4 * j + 2 * a).start()
    mine.wait()
    for j in range(4):
        for a in range(2):
            r = zs[j] * 2 + (x if a == 0 else 1 - x)
            tok(r, col_c, to_core, 0).wait_recv()
            tok(r, col_yc, to_core, 0).wait_recv()

    def wait_weight(part):
        for k in range(1, rows):
            p = (row + k) % rows
            when_held(part, row, lambda p=p: w_copy(row, p, part).wait_recv())
        when_held(part, row, lambda: w_own(part).wait())

    def fetch(i, slot):
        return pltpu.make_async_copy(all_ref.at[(row + 1 + i) % rows], tbuf.at[slot], load.at[slot])

    def o_copy(p, src, part):
        return pltpu.make_async_remote_copy(
            src_ref=staged[part].at[p],
            dst_ref=o_ref.at[:, pl.ds(first_col(src, part), PARTS[part] * LANES)],
            send_sem=osend.at[p * 3 + part],
            recv_sem=orecv.at[src * 3 + part],
            device_id=(p, col),
            device_id_type=MESH,
        )

    def o_own(part):
        return pltpu.make_async_copy(
            staged[part].at[row],
            o_ref.at[:, pl.ds(first_col(row, part), PARTS[part] * LANES)], local.at[4 + part])

    accs = (acc_a, acc_b, acc_c)

    def product(i, slot, part):
        r = (row + 1 + i) % rows
        acc = accs[part]
        acc[...] = jnp.zeros_like(acc)

        def add(k, _):
            block = tbuf[slot, k // 2, :, pl.ds(pl.multiple_of((k % 2) * depth, depth), depth)]
            acc[...] += jnp.dot(block, held[part][k], preferred_element_type=jnp.float32)
            return 0

        lax.fori_loop(0, rows, add, 0)
        staged[part][r] = silu(acc[...]).astype(jnp.bfloat16)

        @pl.when(i < rows - 1)
        def _():
            o_copy(r, row, part).start()

        @pl.when(i == rows - 1)
        def _():
            o_own(part).start()

    for parts in ((0, 2), (1,)):
        for part in parts:
            wait_weight(part)
        fetch(0, 0).start()

        def step(i, _):
            slot = i % 2

            @pl.when(i < rows - 1)
            def _():
                fetch(i + 1, 1 - slot).start()

            fetch(i, slot).wait()
            for part in parts:
                when_held(part, row, lambda part=part: product(i, slot, part))
            return 0

        lax.fori_loop(0, rows, step, 0)

    for part in range(3):
        for k in range(1, rows):
            p = (row + k) % rows
            when_held(part, p, lambda p=p, part=part: w_copy(p, row, part).wait_send())
            when_held(part, row, lambda p=p, part=part: o_copy(p, row, part).wait_send())
            when_held(part, p, lambda p=p, part=part: o_copy(row, p, part).wait_recv())
        when_held(part, row, lambda part=part: o_own(part).wait())
    tok(row, col, to_z, 0).wait_send()
    for slot in range(1, 5):
        @pl.when(inner)
        def _():
            tok(row, col, to_z, slot).wait_send()
    for slot in range(5, 33):
        tok(row, col, to_z, slot).wait_send()


def spread(tokens, weight):
    m, d = tokens.shape
    depth, ff = weight.shape
    bf16, f32 = jnp.bfloat16, jnp.float32
    widths = [n * LANES for n in PARTS]
    out, _ = pl.pallas_call(
        kernel,
        out_shape=(jax.ShapeDtypeStruct((m, ff), bf16), jax.ShapeDtypeStruct((8, 4, m, d), bf16)),
        in_specs=[pl.BlockSpec(memory_space=pl.ANY)] * 2,
        out_specs=[pl.BlockSpec(memory_space=pl.ANY)] * 2,
        scratch_shapes=(
            [pltpu.VMEM((8, depth, n), bf16) for n in widths]
            + [pltpu.VMEM((8, m, n), bf16) for n in widths]
            + [pltpu.VMEM((2, 4, m, d), bf16)]
            + [pltpu.VMEM((m, n), f32) for n in widths]
            + [pltpu.SemaphoreType.DMA((n,)) for n in (33, 32, 24, 24, 24, 24, 7, 2)]
        ),
        compiler_params=pltpu.CompilerParams(
            collective_id=0, has_side_effects=True, vmem_limit_bytes=56 * 2**20),
        cost_estimate=pl.CostEstimate(
            flops=2 * m * 8 * depth * ff, bytes_accessed=2 * 2 * 32 * m * d, transcendentals=m * ff),
    )(tokens, weight)
    return out


def gather(tokens, weight):
    whole_weight = lax.all_gather(weight, "row", axis=0, tiled=True)
    preact = jnp.dot(
        lax.all_gather(tokens, "col", axis=1, tiled=True),
        whole_weight,
        preferred_element_type=jnp.float32,
    )
    return jax.nn.silu(preact).astype(jnp.bfloat16)


def on_device(rows, cols, tokens, weight):
    tiles = 4 * (2 * sum(PARTS[:2]) + 1)
    fits = (rows, cols) == (8, 4) and weight.shape[1] == tiles * LANES and tokens.shape[1] == 2 * weight.shape[0]
    return (spread if fits else gather)(tokens, weight)


def solution(mesh):
    placed = (P("row", "col"), P("row", "col"))
    return jax.shard_map(
        functools.partial(on_device, mesh.shape["row"], mesh.shape["col"]),
        mesh=mesh, in_specs=placed, out_specs=P("row", "col"), check_vma=False,
    )
```

time: 2180 us -> 574 us (0.26)
  waiting for transfers between devices: 2110 us -> 0 us
  Pallas kernels: 0 us -> 565 us
  matrix products: 58.5 us -> 0 us
    all_gather x2 -> x0, waiting for transfers between devices: 2100 us -> none  [the longest x1 2050 us: on_device(): whole_weight = lax.all_gather(weight, 'row', axis=0, tiled=True)]
    pallas_call x0 -> x1, Pallas kernels: none -> 565 us  [spread(): pl.pallas_call(kernel, out_shape=(jax.ShapeDtypeStruct((m, ff), bf16), ja...]
    dot_general x1 -> x0, matrix products: 58.5 us -> none  [on_device(): jnp.dot(lax.all_gather(tokens, 'col', axis=1, tiled=True), whole_weight,...]
  transfers between devices with their start and end apart: 2 -> 0, of which waited for: 2 -> 0; matrix products, arithmetic and copies ran while one was open for 0% -> 0% of each run, Pallas kernels for 0% -> 0%
where the time goes in v1:
time: 574 us; the launch traced here: 570 us
  Pallas kernels  565 us (98%)
    pallas_call x1, Pallas kernels, spread(): pl.pallas_call(kernel, out_shape=(jax.ShapeDtypeStruct((m, ff), bf16), ja...  565 us

profile of v1, /device:TPU:0, one launch (start us, length us, event | category | flops | bytes accessed | tf_op | source)
XLA Modules:
  0.0 570.3 jit_solution(8437269521182835494)
XLA Ops:
  0.0 565.2 %shard_map.28 = (bf16[376,6656]{1,0:T(8,128)(2,1)}, bf16[8,4,376,2048]{3,2,1,0:T(8,128)(2,1)}) custom-call(bf16[376,2048]{1,0:T(8,128)(2,1)} %tok_ref.1, bf16[1024,6656]{1,0:T(8,128)(2,1)} %w_ref.1), custom_call_target="tpu_custom_call" | custom-call | flops 41003515904 | bytes 98566144 | tf_op jit(solution)/shard_map/pallas_call | solution.py:222
  565.3 5.0 copy.4

commit v2 on v1

--- a/solution.py
+++ b/solution.py
@@ -60,19 +60,16 @@
     def z_sends(j):
         r = zs[j] * 2 + x
         own = j == 0
+
+        @pl.when(inner)
+        def _():
+            tok(r, col, to_mid if j < 2 else to_z, 1 + j, own).start()
+
         if own:
             tok(r, col, to_z, 0, own).start()
-        if j < 2:
-            @pl.when(inner)
-            def _():
-                tok(r, col, to_mid, 1 + j, own).start()
-        else:
-            @pl.when(inner)
-            def _():
-                tok(r, col, to_z, 1 + j, own).start()
         tok(r, col, to_x, 5 + j, own).start()
-        tok(r, col, to_y, 9 + 2 * j, own).start()
-        tok(r, col, to_core, 17 + 4 * j, own).start()
+        tok(r, col, to_y, 9 + j, own).start()
+        tok(r, col, to_core, 17 + j, own).start()
 
     mine = pltpu.make_async_copy(tok_ref, all_ref.at[row, col], local.at[0])
     mine.start()
@@ -106,31 +103,25 @@
             w_ref.at[:, pl.ds(first_col(row, part), PARTS[part] * LANES)],
             held[part].at[row], local.at[1 + part])
 
-    for part in (0, 2, 1):
-        for k in (4, 2, 6, 3, 5, 1, 7):
-            p = (row + k) % rows
-            when_held(part, p, lambda p=p, part=part: w_copy(p, row, part).start())
-        when_held(part, row, lambda part=part: w_own(part).start())
-
+    def send_weight(parts, ks):
+        for part in parts:
+            for k in ks:
+                p = (row + k) % rows
+                when_held(part, p, lambda p=p, part=part: w_copy(p, row, part).start())
+
+    for j in range(1, 4):
+        tok(zs[j] * 2 + x, col, to_z, 0).wait_recv()
+        z_sends(j)
+    send_weight((0, 2), (4, 2, 6))
     for j in range(4):
-        if j > 0:
-            tok(zs[j] * 2 + x, col, to_z, 0).wait_recv()
-            z_sends(j)
         r = zs[j] * 2 + 1 - x
         tok(r, col, to_x, 0).wait_recv()
-        tok(r, col, to_y, 10 + 2 * j).start()
-        tok(r, col, to_core, 19 + 4 * j).start()
-    for j in range(4):
-        for a in range(2):
-            r = zs[j] * 2 + (x if a == 0 else 1 - x)
-            tok(r, col_y, to_y, 0).wait_recv()
-            tok(r, col_y, to_core, 18 + 4 * j + 2 * a).start()
-    mine.wait()
-    for j in range(4):
-        for a in range(2):
-            r = zs[j] * 2 + (x if a == 0 else 1 - x)
-            tok(r, col_c, to_core, 0).wait_recv()
-            tok(r, col_yc, to_core, 0).wait_recv()
+        tok(r, col, to_y, 13 + j).start()
+        tok(r, col, to_core, 21 + j).start()
+    send_weight((0, 2), (3, 5, 1, 7))
+    send_weight((1,), (4, 3, 5, 2, 6, 1, 7))
+    for part in range(3):
+        when_held(part, row, lambda part=part: w_own(part).start())
 
     def wait_weight(part):
         for k in range(1, rows):
@@ -138,8 +129,15 @@
             when_held(part, row, lambda p=p: w_copy(row, p, part).wait_recv())
         when_held(part, row, lambda: w_own(part).wait())
 
-    def fetch(i, slot):
-        return pltpu.make_async_copy(all_ref.at[(row + 1 + i) % rows], tbuf.at[slot], load.at[slot])
+    def block(i):
+        late, odd = (i % 4) // 2, i % 2
+        at = (1 - late) * (z + odd * (1 - 2 * (z % 2))) + late * (near + odd * (1 - 2 * half))
+        other = i // 4
+        return at * 2 + x + other * (1 - 2 * x)
+
+    def fetch(i):
+        slot = i % 2
+        return pltpu.make_async_copy(all_ref.at[block(i)], tbuf.at[slot], load.at[slot])
 
     def o_copy(p, src, part):
         return pltpu.make_async_remote_copy(
@@ -158,45 +156,81 @@
 
     accs = (acc_a, acc_b, acc_c)
 
-    def product(i, slot, part):
-        r = (row + 1 + i) % rows
+    def product(i, part):
+        r, slot = block(i), i % 2
         acc = accs[part]
         acc[...] = jnp.zeros_like(acc)
 
         def add(k, _):
-            block = tbuf[slot, k // 2, :, pl.ds(pl.multiple_of((k % 2) * depth, depth), depth)]
-            acc[...] += jnp.dot(block, held[part][k], preferred_element_type=jnp.float32)
+            piece = tbuf[slot, k // 2, :, pl.ds(pl.multiple_of((k % 2) * depth, depth), depth)]
+            acc[...] += jnp.dot(piece, held[part][k], preferred_element_type=jnp.float32)
             return 0
 
         lax.fori_loop(0, rows, add, 0)
         staged[part][r] = silu(acc[...]).astype(jnp.bfloat16)
 
+        @pl.when(i > 0)
+        def _():
+            o_copy(r, row, part).start()
+
+        @pl.when(i == 0)
+        def _():
+            o_own(part).start()
+
+    def multiply(i, parts):
+        fetch(i).wait()
+        for part in parts:
+            when_held(part, row, lambda part=part: product(i, part))
+
+    lag = 5
+
+    def first(i, _):
+        @pl.when(i < rows)
+        def _():
+            r = block(i)
+            tok(r, col_y, to_y, 0).wait_recv()
+            tok(r, col_y, to_core, 25 + i).start()
+
+        @pl.when(i == lag)
+        def _():
+            mine.wait()
+            wait_weight(0)
+            wait_weight(2)
+
+        @pl.when((i >= lag - 1) & (i < rows + lag - 1))
+        def _():
+            r = block(i - lag + 1)
+            tok(r, col_c, to_core, 0).wait_recv()
+            tok(r, col_yc, to_core, 0).wait_recv()
+
+        @pl.when((i >= lag) & (i < rows + lag - 1))
+        def _():
+            fetch(i - lag + 1).start()
+
+        @pl.when(i == lag)
+        def _():
+            fetch(0).start()
+
+        @pl.when(i >= lag)
+        def _():
+            multiply(i - lag, (0, 2))
+
+        return 0
+
+    lax.fori_loop(0, rows + lag, first, 0)
+
+    wait_weight(1)
+    fetch(0).start()
+
+    def second(i, _):
         @pl.when(i < rows - 1)
         def _():
-            o_copy(r, row, part).start()
-
-        @pl.when(i == rows - 1)
-        def _():
-            o_own(part).start()
-
-    for parts in ((0, 2), (1,)):
-        for part in parts:
-            wait_weight(part)
-        fetch(0, 0).start()
-
-        def step(i, _):
-            slot = i % 2
-
-            @pl.when(i < rows - 1)
-            def _():
-                fetch(i + 1, 1 - slot).start()
-
-            fetch(i, slot).wait()
-            for part in parts:
-                when_held(part, row, lambda part=part: product(i, slot, part))
-            return 0
-
-        lax.fori_loop(0, rows, step, 0)
+            fetch(i + 1).start()
+
+        multiply(i, (1,))
+        return 0
+
+    lax.fori_loop(0, rows, second, 0)
 
     for part in range(3):
         for k in range(1, rows):

time: 574 us -> 493 us (0.86)
  Pallas kernels: 565 us -> 487 us
    pallas_call x1, Pallas kernels: 565 us -> 487 us  [spread(): pl.pallas_call(kernel, out_shape=(jax.ShapeDtypeStruct((m, ff), bf16), ja...]
where the time goes in v2:
time: 493 us; the launch traced here: 492 us
  Pallas kernels  487 us (99%)
  local copies, waits for them, and re-layouts  5.02 us (1%)
    pallas_call x1, Pallas kernels, spread(): pl.pallas_call(kernel, out_shape=(jax.ShapeDtypeStruct((m, ff), bf16), ja...  487 us

profile of v2, /device:TPU:0, one launch (start us, length us, event | category | flops | bytes accessed | tf_op | source)
XLA Modules:
  0.0 492.3 jit_solution(4225161336805697005)
XLA Ops:
  0.0 487.3 %shard_map.28 = (bf16[376,6656]{1,0:T(8,128)(2,1)}, bf16[8,4,376,2048]{3,2,1,0:T(8,128)(2,1)}) custom-call(bf16[376,2048]{1,0:T(8,128)(2,1)} %tok_ref.1, bf16[1024,6656]{1,0:T(8,128)(2,1)} %w_ref.1), custom_call_target="tpu_custom_call" | custom-call | flops 41003515904 | bytes 98566144 | tf_op jit(solution)/shard_map/pallas_call | solution.py:256
  487.3 5.0 %copy.4 = bf16[376,6656]{1,0:T(8,128)(2,1)} copy(bf16[376,6656]{1,0:T(8,128)(2,1)} %get-tuple-element.6) | data formatting | bytes 10010624

commit v3 on v2

--- a/solution.py
+++ b/solution.py
@@ -9,7 +9,7 @@
 
 LANES = 128
 MESH = pl.DeviceIdType.MESH
-PARTS = (4, 2, 1)
+PARTS = (5, 1, 1)
 
 
 def silu(v):
@@ -135,9 +135,12 @@
         other = i // 4
         return at * 2 + x + other * (1 - 2 * x)
 
-    def fetch(i):
+    def far_first(i):
+        return i % 2 + 4 * (i % 4 // 2) + 2 * (1 - i // 4)
+
+    def fetch(i, n):
         slot = i % 2
-        return pltpu.make_async_copy(all_ref.at[block(i)], tbuf.at[slot], load.at[slot])
+        return pltpu.make_async_copy(all_ref.at[block(n)], tbuf.at[slot], load.at[slot])
 
     def o_copy(p, src, part):
         return pltpu.make_async_remote_copy(
@@ -156,8 +159,8 @@
 
     accs = (acc_a, acc_b, acc_c)
 
-    def product(i, part):
-        r, slot = block(i), i % 2
+    def product(i, n, part):
+        r, slot = block(n), i % 2
         acc = accs[part]
         acc[...] = jnp.zeros_like(acc)
 
@@ -169,18 +172,18 @@
         lax.fori_loop(0, rows, add, 0)
         staged[part][r] = silu(acc[...]).astype(jnp.bfloat16)
 
-        @pl.when(i > 0)
+        @pl.when(n > 0)
         def _():
             o_copy(r, row, part).start()
 
-        @pl.when(i == 0)
+        @pl.when(n == 0)
         def _():
             o_own(part).start()
 
-    def multiply(i, parts):
-        fetch(i).wait()
+    def multiply(i, n, parts):
+        fetch(i, n).wait()
         for part in parts:
-            when_held(part, row, lambda part=part: product(i, part))
+            when_held(part, row, lambda part=part: product(i, n, part))
 
     lag = 5
 
@@ -205,29 +208,29 @@
 
         @pl.when((i >= lag) & (i < rows + lag - 1))
         def _():
-            fetch(i - lag + 1).start()
+            fetch(i - lag + 1, i - lag + 1).start()
 
         @pl.when(i == lag)
         def _():
-            fetch(0).start()
+            fetch(0, 0).start()
 
         @pl.when(i >= lag)
         def _():
-            multiply(i - lag, (0, 2))
+            multiply(i - lag, i - lag, (0, 2))
 
         return 0
 
     lax.fori_loop(0, rows + lag, first, 0)
 
+    fetch(0, far_first(0)).start()
     wait_weight(1)
-    fetch(0).start()
 
     def second(i, _):
         @pl.when(i < rows - 1)
         def _():
-            fetch(i + 1).start()
-
-        multiply(i, (1,))
+            fetch(i + 1, far_first(i + 1)).start()
+
+        multiply(i, far_first(i), (1,))
         return 0
 
     lax.fori_loop(0, rows, second, 0)

time: 493 us -> 486 us (0.986)
  Pallas kernels: 487 us -> 480 us
    pallas_call x1, Pallas kernels: 487 us -> 480 us  [spread(): pl.pallas_call(kernel, out_shape=(jax.ShapeDtypeStruct((m, ff), bf16), ja...]
where the time goes in v3:
time: 486 us; the launch traced here: 485 us
  Pallas kernels  480 us (99%)
  local copies, waits for them, and re-layouts  5.02 us (1%)
    pallas_call x1, Pallas kernels, spread(): pl.pallas_call(kernel, out_shape=(jax.ShapeDtypeStruct((m, ff), bf16), ja...  480 us

profile of v3, /device:TPU:0, one launch (start us, length us, event | category | flops | bytes accessed | tf_op | source)
XLA Modules:
  0.0 485.3 jit_solution(18346328371117453504)
XLA Ops:
  0.0 480.3 %shard_map.28 = (bf16[376,6656]{1,0:T(8,128)(2,1)}, bf16[8,4,376,2048]{3,2,1,0:T(8,128)(2,1)}) custom-call(bf16[376,2048]{1,0:T(8,128)(2,1)} %tok_ref.1, bf16[1024,6656]{1,0:T(8,128)(2,1)} %w_ref.1), custom_call_target="tpu_custom_call" | custom-call | flops 41003515904 | bytes 98566144 | tf_op jit(solution)/shard_map/pallas_call | solution.py:259
  480.3 5.0 %copy.4 = bf16[376,6656]{1,0:T(8,128)(2,1)} copy(bf16[376,6656]{1,0:T(8,128)(2,1)} %get-tuple-element.6) | data formatting | bytes 10010624
